TPU v7x, 512 devices: a whole 4x8x8 slice. The times are simulated.
512 devices in a mesh: inp: 128 (over y, z_hi, x, core), tm: 4 (over z_lo).
Axes of the slice: x: 4, y: 8, z: 8 (z_hi: 2, z_lo: 4; z = z_hi * 4 + z_lo), core: 2. Of those that a mesh axis runs over, the one named last changes fastest.
Arguments:
- raw_samples: bfloat16 [1024, 262144], P('inp', 'tm'), may hold values from -6 to 6
- filter_taps: float32 [4, 2048], replicated, may hold values from -3 to 3
Outputs:
- visibilities: float32 [128, 1024, 1024], P('inp', 'tm')
All inputs are finite; a program needn't handle non-finite values.
Results may differ from a plain program's by a relative error of at most 0.014.
Values may be sent and summed in bfloat16 or wider, within the bound.
A program may use at most 64 MiB of HBM per device.

v0:
```python
import math

import jax
import jax.numpy as jnp
from jax import lax
from jax.sharding import PartitionSpec as P

NFFT = 2048


def from_behind(value, axis, steps):
    count = lax.axis_size(axis)
    first, last = (max(0, -steps), min(count, count - steps))
    return lax.ppermute(value, axis, [(source, source + steps) for source in range(first, last)])


def fourier_table(length, channels):
    sample_index = jnp.arange(length, dtype=jnp.int32)[:, None]
    channel_index = jnp.arange(1, channels + 1, dtype=jnp.int32)[None, :]
    angles = (sample_index * channel_index % length).astype(jnp.float32) * (2.0 * math.pi / length)
    return jnp.concatenate([jnp.cos(angles), -jnp.sin(angles)], axis=1).astype(jnp.bfloat16)


def polyphase(frames, filter_taps, earlier):
    taps = filter_taps.shape[0]
    frame_count = frames.shape[1]
    padded = jnp.concatenate([earlier, frames], axis=1).astype(jnp.float32)
    running = jnp.zeros(frames.shape, jnp.float32)
    for tap_index in range(taps):
        begin = taps - 1 - tap_index
        running = running + filter_taps[tap_index] * padded[:, begin : begin + frame_count, :]
    return running.astype(jnp.bfloat16)


def pack_triangle(real_part, imag_part, row_offset):
    row_index = row_offset + jnp.arange(real_part.shape[0], dtype=jnp.int32)[:, None]
    col_index = jnp.arange(real_part.shape[1], dtype=jnp.int32)[None, :]
    return jnp.where(row_index <= col_index, real_part, imag_part)


def contract(left, right):
    return lax.dot_general(
        left, right, (((1,), (1,)), ((), ())), preferred_element_type=jnp.float32
    )


def operands(spectra):
    real_part, imag_part = (spectra[0], spectra[1])
    stacked = jnp.concatenate([real_part, imag_part], axis=1)
    rotated = jnp.concatenate([imag_part, -real_part], axis=1)
    return (stacked, rotated)


def packed_rows(stacked, rotated, offset, length):
    stack_rows = lax.dynamic_slice_in_dim(stacked, offset, length, 0)
    rotate_rows = lax.dynamic_slice_in_dim(rotated, offset, length, 0)
    both_rows = jnp.concatenate([stack_rows, rotate_rows], axis=0)
    product = contract(both_rows, stacked)
    return pack_triangle(product[:length], product[length:], offset)


def body(raw_samples, filter_taps):
    taps = filter_taps.shape[0]
    inp_dev = raw_samples.shape[0]
    local_count = raw_samples.shape[1] // NFFT
    frames = raw_samples.reshape(inp_dev, local_count, NFFT)
    earlier = from_behind(frames[:, local_count - (taps - 1) :, :], "tm", 1)
    filtered = polyphase(frames, filter_taps, earlier)
    channels = lax.axis_size("inp")
    table = fourier_table(NFFT, channels)
    spectra = jnp.einsum("ifn,nk->kif", filtered, table, preferred_element_type=jnp.float32)
    spectra = (spectra * (1.0 / math.sqrt(NFFT))).astype(jnp.bfloat16)
    spectra = spectra.reshape(2, channels, inp_dev, local_count)
    turned = lax.all_to_all(spectra, "inp", split_axis=1, concat_axis=2, tiled=True)[:, 0]
    all_inputs = turned.shape[1]
    groups = lax.axis_size("tm")
    row_count = all_inputs // groups
    inverse = jnp.float32(1.0 / (local_count * groups))
    stacked, rotated = operands(turned)
    offset = jnp.int32(0)
    blocks = [
        packed_rows(stacked, rotated, offset + segment * row_count, row_count)
        for segment in range(lax.axis_size("tm") * row_count // row_count)
    ]
    visibilities = lax.psum_scatter(
        (jnp.concatenate(blocks, axis=0) * inverse).astype(jnp.bfloat16),
        "tm",
        scatter_dimension=0,
        tiled=True,
    ).astype(jnp.float32)
    return visibilities[None]


def solution(mesh):
    placed = (P("inp", "tm"), P())
    return jax.shard_map(
        body, mesh=mesh, in_specs=placed, out_specs=P("inp", "tm", None), check_vma=False
    )
```

profile of v0, /device:TPU:1, one launch (start us, length us, event | category | flops | bytes accessed | tf_op | source)
XLA Modules:
  0.0 113.6 jit_solution(6833218401910216015)
XLA Ops:
  6.5 0.0 copy-start
  6.5 1.8 %copy.8 = bf16[8,32,2048]{2,1,0:T(8,128)(2,1)S(1)} copy(bf16[8,32,2048]{2,0,1:T(8,128)(2,1)} %bitcast.24) | data formatting | bytes 2097152 | tf_op jit(solution)/shard_map/reshape | solution.py:66
  8.3 0.1 slice.79
  8.4 4.8 %collective-permute-start = (bf16[8,3,2048]{2,1,0:T(4,128)(2,1)S(1)}, bf16[8,3,2048]{2,1,0:T(4,128)(2,1)S(1)}, u32[]{:S(2)}, u32[]{:S(2)}) collective-permute-start(bf16[8,3,2048]{2,1,0:T(4,128)(2,1)S(1)} %slice.79), channel_id=1, source_target_pairs={{0,1},{1,2},{2,3},{4,5},{5,6},{6,7},{8,9},{9,10},{10,11},{12,13},{... | collective-permute-start | bytes 294920 | tf_op jit(solution)/shard_map/ppermute | solution.py:14
  13.3 4.4 %cosine_convert_fusion = (bf16[2048,128]{1,0:T(8,128)(2,1)S(1)}, bf16[2048,128]{1,0:T(8,128)(2,1)S(1)}) fusion(s32[128]{0:T(128)S(1)} %iota_add_fusion.3), kind=kLoop, calls=%fused_computation.30 | loop fusion | flops 4456448 | bytes 1049088 | tf_op jit(solution)/shard_map/convert.1
  17.7 0.0 copy-done
  17.8 0.0 collective-permute-done
  17.8 0.4 maximum_convert_fusion
  18.2 1.0 fusion.5
  19.3 0.4 copy.10
  19.7 1.0 reshape.43
  20.7 19.4 %all-to-all-start = ((bf16[128,2,256]{2,1,0:T(2,128)(2,1)}), bf16[128,2,256]{2,1,0:T(2,128)(2,1)S(1)}, u32[]{:S(2)}, u32[]{:S(2)}) async-start(bf16[128,2,256]{2,1,0:T(2,128)(2,1)} %reshape.43), calls=%async_computation | async-start | bytes 262144 | tf_op jit(solution)/shard_map/all_to_all | solution.py:74
  40.1 0.0 reduce-scatter.2.cloned.1.call-start
  40.2 15.9 %all-to-all-done = bf16[128,2,256]{2,1,0:T(2,128)(2,1)S(1)} async-done(((bf16[128,2,256]{2,1,0:T(2,128)(2,1)}), bf16[128,2,256]{2,1,0:T(2,128)(2,1)S(1)}, u32[]{:S(2)}, u32[]{:S(2)}) %all-to-all-start) | async-done | bytes 131104 | tf_op jit(solution)/shard_map/all_to_all | solution.py:74
  56.1 0.3 reshape.44
  56.5 0.3 fusion.38
  56.8 0.5 fusion.19
  57.3 0.5 fusion.33
  57.8 0.5 fusion.29
  58.4 0.5 fusion.25
  58.9 0.3 slice_select_fusion.2
  59.1 0.3 slice_select_fusion
  59.4 1.9 %fusion = bf16[1024,1024]{1,0:T(8,128)(2,1)} fusion(f32[256,1024]{1,0:T(8,128)S(1)} %get-tuple-element.23, f32[256,1024]{1,0:T(8,128)S(1)} %get-tuple-element.24, f32[256,1024]{1,0:T(8,128)S(1)} %get-tuple-element.25, f32[256,1024]{1,0:T(8,128)S(1)} %get-tuple-element.26), kind=kLoop, calls=%fused_computation.1 | loop fusion | flops 5242880 | bytes 6291456 | tf_op jit(solution)/shard_map/convert_element_type | solution.py:86
  61.3 0.0 reduce-scatter.2.cloned.1.call-update
  61.4 43.3 %reduce-scatter.2.cloned.1.call-done = bf16[256,1024]{1,0:T(8,128)(2,1)} async-done(((bf16[1024,1024]{1,0:T(8,128)(2,1)}), bf16[256,1024]{1,0:T(8,128)(2,1)}) %reduce-scatter.2.cloned.1.call-update) | async-done | bytes 524304 | tf_op jit(solution)/shard_map/reduce_scatter | solution.py:85
  104.7 2.1 %bitcast_convert_fusion = f32[1,256,1024]{2,1,0:T(8,128)} fusion(bf16[256,1024]{1,0:T(8,128)(2,1)} %reduce-scatter.2.cloned.1.call-done), kind=kLoop, calls=%fused_computation.35 | loop fusion | flops 262144 | bytes 1572864 | tf_op jit(solution)/shard_map/broadcast_in_dim | solution.py:91
  (8 shorter events, 0.2 us)
Async XLA Ops:
  6.5 11.2 %copy-start = (f32[4,2048]{1,0:T(4,128)S(1)}, f32[4,2048]{1,0:T(4,128)}, u32[]{:S(2)}) copy-start(f32[4,2048]{1,0:T(4,128)} %param.3) | copy-start | bytes 98308
  8.4 9.3 %collective-permute-start = (bf16[8,3,2048]{2,1,0:T(4,128)(2,1)S(1)}, bf16[8,3,2048]{2,1,0:T(4,128)(2,1)S(1)}, u32[]{:S(2)}, u32[]{:S(2)}) collective-permute-start(bf16[8,3,2048]{2,1,0:T(4,128)(2,1)S(1)} %slice.79), channel_id=1, source_target_pairs={{0,1},{1,2},{2,3},{4,5},{5,6},{6,7},{8,9},{9,10},{10,11},{12,13},{... | collective-permute-start | bytes 294920 | tf_op jit(solution)/shard_map/ppermute | solution.py:14
  20.7 35.4 %all-to-all-start = ((bf16[128,2,256]{2,1,0:T(2,128)(2,1)}), bf16[128,2,256]{2,1,0:T(2,128)(2,1)S(1)}, u32[]{:S(2)}, u32[]{:S(2)}) async-start(bf16[128,2,256]{2,1,0:T(2,128)(2,1)} %reshape.43), calls=%async_computation | async-start | bytes 262144 | tf_op jit(solution)/shard_map/all_to_all | solution.py:74
  40.1 64.5 %reduce-scatter.2.cloned.1.call-start = ((), (), s32[]{:S(2)}) async-start(), calls=%async_computation.2 | async-start | bytes 2621440 | tf_op jit(solution)/shard_map/reduce_scatter | solution.py:85
Sparse Core Ops, SparseCore 0:
  61.5 43.1 reduce-scatter.1
where the time goes:
time: 114 us
  waiting for transfers between devices  59.2 us (52%)
  starting transfers between devices  24.3 us (21%)
  between operations  13.6 us (12%)
  other arithmetic  9.72 us (9%)
  local copies, waits for them, and re-layouts  3.72 us (3%)
  matrix products  3.09 us (3%)
    reduce_scatter x1, waiting for transfers between devices, body(): lax.psum_scatter((jnp.concatenate(blocks, axis=0) * inverse).astype(jnp.b...  43.3 us
    all_to_all x1, starting transfers between devices, body(): lax.all_to_all(spectra, 'inp', split_axis=1, concat_axis=2, tiled=True)  19.4 us
    all_to_all x1, waiting for transfers between devices, body(): lax.all_to_all(spectra, 'inp', split_axis=1, concat_axis=2, tiled=True)  15.9 us
    ppermute x1, starting transfers between devices, from_behind(): lax.ppermute(value, axis, [(source, source + steps) for source in range(f...  4.83 us
    another operation x1, other arithmetic  4.44 us
  transfers between devices with their start and end apart: 3, of which 2 were waited for; matrix products, arithmetic and copies ran while one was open for 4% of the time, Pallas kernels for 0%

commit v1 on v0

v1 whole, which is shorter than its diff:
```python
import math

import jax
import jax.numpy as jnp
import numpy as np
from jax import lax
from jax.experimental import pallas as pl
from jax.experimental.pallas import tpu as pltpu
from jax.sharding import PartitionSpec as P

MESH = pl.DeviceIdType.MESH
NFFT = 2048
TAPS = 4
FRAMES = 32
ALL_FRAMES = 128
PLANE = 64
LANES = 128
CHUNK = 512
SCALE = 1.0 / math.sqrt(NFFT)


def table_rows():
    row = np.arange(4 * PLANE)
    part, z_hi, dest = row % 2, row // 2 % 2, row // 4
    channel = ((dest // 8) * 2 + z_hi) * 8 + dest % 8
    n = np.arange(NFFT)
    m = (n[None, :] * (channel[:, None] + 1)) % NFFT
    angles = m.astype(np.float32) * np.float32(2.0 * math.pi / NFFT)
    rows = np.where(part[:, None] == 0, np.cos(angles), -np.sin(angles))
    return rows.astype(np.float32).astype(jnp.bfloat16)


def nt(left, right):
    return lax.dot_general(
        left, right, (((1,), (1,)), ((), ())), preferred_element_type=jnp.float32
    )


def nn(left, right):
    return lax.dot_general(
        left, right, (((1,), (0,)), ((), ())), preferred_element_type=jnp.float32
    )


def filter_frames(first, last, taps_v, raw_v, halo_v, filt_v):
    def step(c, carry):
        base = pl.multiple_of(c * CHUNK, CHUNK)
        taps = [taps_v[k : k + 1, pl.ds(base, CHUNK)] for k in range(TAPS)]

        def frame(f):
            if f < 0:
                ref, at = halo_v, (f + TAPS - 1) * NFFT
            else:
                ref, at = raw_v, f * NFFT
            at = pl.multiple_of(base + at, CHUNK)
            return ref[:, pl.ds(at, CHUNK)].astype(jnp.float32)

        window = [frame(first - k) for k in range(TAPS)]
        done = []
        for f in range(first, last):
            if f > first:
                window = [frame(f)] + window[: TAPS - 1]
            total = taps[0] * window[0]
            for k in range(1, TAPS):
                total = total + taps[k] * window[k]
            done.append(total)
            if len(done) == 2:
                pair = jnp.concatenate(done, axis=0).astype(jnp.bfloat16)
                filt_v[(f - 1) * 8 : (f + 1) * 8, pl.ds(base, CHUNK)] = pair
                done = []
        return carry

    lax.fori_loop(0, NFFT // CHUNK, step, 0)


def turn(rows):
    lane = lax.broadcasted_iota(jnp.int32, (8, LANES), 1)
    for b in range(4):
        step, width = 1 << b, 8 << b
        low = (lane & width) == 0
        out = list(rows)
        for s in range(16):
            if s & step == 0:
                x, y = rows[s], rows[s + step]
                out[s] = jnp.where(low, x, pltpu.roll(y, width, 1))
                out[s + step] = jnp.where(low, pltpu.roll(x, LANES - width, 1), y)
        rows = out
    return rows


def kernel(
    raw, taps, table, out,
    raw_v, taps_v, table_v, halo_v, filt_v, sbuf, rbuf, xs, xr, lt,
    in_sem, halo_ssem, halo_rsem, ssem, rsem, zssem, zrsem,
):
    me = lax.axis_index("inp")
    t = lax.axis_index("tm")
    y, zh, xc = me // 16, (me // 8) % 2, me % 8
    mine = y * 8 + xc
    my_m, my_lo = mine // 16, mine % 16
    my_z = zh * 4 + t

    def plane(d):
        return ((d // 8) * 16 + zh * 8 + d % 8, t)

    def column(z):
        return (y * 16 + (z // 4) * 8 + xc, z % 4)

    loads = [
        pltpu.make_async_copy(table, table_v, in_sem.at[0]),
        pltpu.make_async_copy(taps, taps_v, in_sem.at[1]),
        pltpu.make_async_copy(raw, raw_v, in_sem.at[2]),
    ]
    for load in loads:
        load.start()

    barrier = pltpu.get_barrier_semaphore()
    for k in range(1, 8):
        pl.semaphore_signal(
            barrier, inc=1, device_id=column((my_z + k) % 8), device_id_type=MESH
        )

    def greet(k, carry):
        pl.semaphore_signal(
            barrier, inc=1, device_id=plane((mine + k) % PLANE), device_id_type=MESH
        )
        return carry

    lax.fori_loop(1, PLANE, greet, 0)
    pl.semaphore_wait(barrier, PLANE - 1 + 7)

    halo = pltpu.make_async_remote_copy(
        src_ref=raw.at[:, pl.ds((FRAMES - TAPS + 1) * NFFT, (TAPS - 1) * NFFT)],
        dst_ref=halo_v,
        send_sem=halo_ssem,
        recv_sem=halo_rsem,
        device_id=(me, (t + 1) % 4),
        device_id_type=MESH,
    )

    @pl.when(t < 3)
    def _():
        halo.start()

    for load in loads:
        load.wait()
    filter_frames(4, FRAMES, taps_v, raw_v, halo_v, filt_v)
    s1 = nt(table_v[...], filt_v[LANES:, :])

    @pl.when(t > 0)
    def _():
        halo.wait_recv()

    @pl.when(t == 0)
    def _():
        halo_v[...] = jnp.zeros_like(halo_v)

    filter_frames(0, 4, taps_v, raw_v, halo_v, filt_v)
    s0 = nt(table_v[...], filt_v[:LANES, :])
    s0 = (s0 * SCALE).reshape(PLANE // 2, 8, LANES)
    s1 = (s1 * SCALE).reshape(PLANE // 2, 8, LANES)
    first = lax.broadcasted_iota(jnp.int32, (PLANE // 2, 8, LANES), 1) < 4
    sbuf[:, 0] = jnp.where(first, s0, pltpu.roll(s1, 4, 1)).astype(jnp.bfloat16)
    sbuf[:, 1] = jnp.where(first, pltpu.roll(s0, 4, 1), s1).astype(jnp.bfloat16)

    own = pltpu.make_async_copy(
        sbuf.at[mine // 2, mine % 2], rbuf.at[mine], rsem.at[my_m]
    )
    own.start()

    def send(k, carry):
        d = ((my_m + k // 16) % 4) * 16 + (my_lo + k % 16) % 16
        pltpu.make_async_remote_copy(
            src_ref=sbuf.at[d // 2, d % 2],
            dst_ref=rbuf.at[mine],
            send_sem=ssem,
            recv_sem=rsem.at[my_m],
            device_id=plane(d),
            device_id_type=MESH,
        ).start()
        return carry

    lax.fori_loop(1, PLANE, send, 0)

    sub = lax.broadcasted_iota(jnp.int32, (8, LANES), 0)

    def relay(j, carry):
        m = (my_m - j + 4) % 4
        got = rbuf.at[pl.ds(m * 16, 16)]
        pltpu.make_async_copy(got, got, rsem.at[m]).wait()
        rows = turn([rbuf[m * 16 + s].astype(jnp.float32) for s in range(16)])
        halves = ([], [])
        for p in range(8):
            a, b = rows[2 * p], rows[2 * p + 1]
            halves[0].append(jnp.where((sub & 2) == 0, a, pltpu.roll(b, 2, 0)))
            halves[1].append(jnp.where((sub & 2) == 0, pltpu.roll(a, 6, 0), b))
        for h in range(2):
            for q in range(4):
                pair = jnp.concatenate(halves[h][2 * q : 2 * q + 2], axis=0)
                xs[m, h, 16 * q : 16 * q + 16, :] = pair.astype(jnp.bfloat16)
        pltpu.make_async_copy(xs.at[m, zh], xr.at[m, my_z], zrsem.at[m]).start()
        for k in (4, 3, 5, 2, 6, 1, 7):
            z = (my_z + k) % 8
            pltpu.make_async_remote_copy(
                src_ref=xs.at[m, z // 4],
                dst_ref=xr.at[m, my_z],
                send_sem=zssem.at[m],
                recv_sem=zrsem.at[m],
                device_id=column(z),
                device_id_type=MESH,
            ).start()
        return carry

    lax.fori_loop(0, 4, relay, 0)

    for m in range(4):
        pltpu.make_async_copy(xr.at[m], xr.at[m], zrsem.at[m]).wait()

    def block(m):
        both = [xr[m, 4 * z : 4 * z + 4].reshape(256, LANES) for z in range(2)]
        return jnp.concatenate(both, axis=1)

    held = block(t).astype(jnp.float32)
    grouped = held.reshape(32, 8, 256)
    even = lax.broadcasted_iota(jnp.int32, (32, 8, 256), 1) % 2 == 0
    swapped = jnp.where(even, pltpu.roll(grouped, 7, 1), -pltpu.roll(grouped, 1, 1))
    lt[0] = held.T.astype(jnp.bfloat16)
    lt[1] = swapped.reshape(256, 256).T.astype(jnp.bfloat16)

    lane = lax.broadcasted_iota(jnp.int32, (256, LANES), 1)

    def put(m, packed):
        packed = packed * (1.0 / ALL_FRAMES)
        a, b = packed[:, :LANES], packed[:, LANES:]
        base = pl.multiple_of(m * 256, 256)
        tiles = (
            jnp.where(lane < 64, a, pltpu.roll(b, 64, 1)),
            jnp.where(lane < 64, pltpu.roll(a, 64, 1), b),
        )
        for part, tile in enumerate(tiles):
            for z in range(2):
                for half in range(2):
                    out[
                        half * 128 + z * 64 : half * 128 + z * 64 + 64,
                        pl.ds(base + part * LANES, LANES),
                    ] = tile[z * 128 + half * 64 : z * 128 + half * 64 + 64]

    def place(index):
        return (index // 64 % 2) * 128 + (index // 128) * 64 + index % 64

    right = block(t)
    row = place(lax.broadcasted_iota(jnp.int32, (256, 256), 0))
    col = place(lax.broadcasted_iota(jnp.int32, (256, 256), 1))
    put(t, jnp.where(row <= col, nn(lt[0], right), nn(lt[1], right)))

    def other(j, carry):
        m = (t + j) % 4
        put(m, nn(lt[(m < t).astype(jnp.int32)], block(m)))
        return carry

    lax.fori_loop(1, 4, other, 0)

    @pl.when(t < 3)
    def _():
        halo.wait_send()

    sent = rbuf.at[pl.ds(0, PLANE - 1)]
    pltpu.make_async_copy(sent, sent, ssem).wait()
    for m in range(4):
        sent = xr.at[m, pl.ds(0, 7)]
        pltpu.make_async_copy(sent, sent, zssem.at[m]).wait()


def body(raw_samples, filter_taps):
    anywhere = pl.BlockSpec(memory_space=pl.ANY)
    visibilities = pl.pallas_call(
        kernel,
        out_shape=jax.ShapeDtypeStruct((256, 1024), jnp.float32),
        in_specs=[anywhere] * 3,
        out_specs=pl.BlockSpec(memory_space=pltpu.VMEM),
        scratch_shapes=[
            pltpu.VMEM((8, FRAMES * NFFT), jnp.bfloat16),
            pltpu.VMEM((TAPS, NFFT), jnp.float32),
            pltpu.VMEM((4 * PLANE, NFFT), jnp.bfloat16),
            pltpu.VMEM((8, (TAPS - 1) * NFFT), jnp.bfloat16),
            pltpu.VMEM((8 * FRAMES, NFFT), jnp.bfloat16),
            pltpu.VMEM((PLANE // 2, 2, 8, LANES), jnp.bfloat16),
            pltpu.VMEM((PLANE, 8, LANES), jnp.bfloat16),
            pltpu.VMEM((4, 2, 64, LANES), jnp.bfloat16),
            pltpu.VMEM((4, 8, 64, LANES), jnp.bfloat16),
            pltpu.VMEM((2, 256, 256), jnp.bfloat16),
            pltpu.SemaphoreType.DMA((3,)),
            pltpu.SemaphoreType.DMA,
            pltpu.SemaphoreType.DMA,
            pltpu.SemaphoreType.DMA,
            pltpu.SemaphoreType.DMA((4,)),
            pltpu.SemaphoreType.DMA((4,)),
            pltpu.SemaphoreType.DMA((4,)),
        ],
        compiler_params=pltpu.CompilerParams(
            collective_id=0, has_side_effects=True, vmem_limit_bytes=40 << 20
        ),
    )(raw_samples, filter_taps, jnp.asarray(table_rows()))
    return visibilities[None]


def solution(mesh):
    return jax.shard_map(
        body,
        mesh=mesh,
        in_specs=(P("inp", "tm"), P()),
        out_specs=P("inp", "tm", None),
        check_vma=False,
    )
```

time: 114 us -> 45.3 us (0.40)
  waiting for transfers between devices: 59.2 us -> 0 us
  Pallas kernels: 0 us -> 40.9 us
  starting transfers between devices: 24.3 us -> 0 us
  between operations: 13.6 us -> 0.01 us
  other arithmetic: 9.72 us -> 0 us
  matrix products: 3.09 us -> 0 us
    reduce_scatter x1 -> x0, waiting for transfers between devices: 43.3 us -> none  [body(): lax.psum_scatter((jnp.concatenate(blocks, axis=0) * inverse).astype(jnp.b...]
    pallas_call x0 -> x1, Pallas kernels: none -> 40.9 us  [body(): pl.pallas_call(kernel, out_shape=jax.ShapeDtypeStruct((256, 1024), jnp.fl...]
    all_to_all x1 -> x0, starting transfers between devices: 19.4 us -> none  [body(): lax.all_to_all(spectra, 'inp', split_axis=1, concat_axis=2, tiled=True)]
    all_to_all x1 -> x0, waiting for transfers between devices: 15.9 us -> none  [body(): lax.all_to_all(spectra, 'inp', split_axis=1, concat_axis=2, tiled=True)]
    ppermute x1 -> x0, starting transfers between devices: 4.83 us -> none  [from_behind(): lax.ppermute(value, axis, [(source, source + steps) for source in range(f...]
    another operation x1 -> x0, other arithmetic: 4.44 us -> none
    dot_general x5 -> x0, matrix products: 3.09 us -> none  [the longest x4 2.07 us: contract(): lax.dot_general(left, right, (((1,), (1,)), ((), ())), preferred_element_...]
    unnamed x4 -> x7, local copies, waits for them, and re-layouts: 1.3 us -> 4.18 us
  transfers between devices with their start and end apart: 3 -> 0, of which waited for: 2 -> 0; matrix products, arithmetic and copies ran while one was open for 4% -> 0% of each run, Pallas kernels for 0% -> 0%
where the time goes in v1:
time: 45.3 us; the launch traced here: 45 us
  Pallas kernels  40.9 us (90%)
  local copies, waits for them, and re-layouts  4.18 us (9%)
    pallas_call x1, Pallas kernels, body(): pl.pallas_call(kernel, out_shape=jax.ShapeDtypeStruct((256, 1024), jnp.fl...  40.9 us
    unnamed x7, local copies, waits for them, and re-layouts  4.18 us

profile of v1, /device:TPU:1, one launch (start us, length us, event | category | flops | bytes accessed | tf_op | source)
XLA Modules:
  0.0 45.0 jit_solution(12798650299040705807)
XLA Ops:
  0.0 0.0 copy-start
  0.0 1.2 %copy-done = bf16[8,65536]{1,0:T(8,128)(2,1)S(1)} copy-done((bf16[8,65536]{1,0:T(8,128)(2,1)S(1)}, bf16[8,65536]{1,0:T(8,128)(2,1)}, u32[]{:S(2)}) %copy-start) | copy-done | bytes 1048600
  1.2 0.0 copy-start.1
  1.2 1.2 %copy-done.1 = bf16[256,2048]{1,0:T(8,128)(2,1)S(1)} copy-done((bf16[256,2048]{1,0:T(8,128)(2,1)S(1)}, bf16[256,2048]{1,0:T(8,128)(2,1)}, u32[]{:S(2)}) %copy-start.1) | copy-done | bytes 1048600
  2.5 0.0 copy-start.2
  2.5 0.8 %copy-done.2 = f32[4,2048]{1,0:T(4,128)S(1)} copy-done((f32[4,2048]{1,0:T(4,128)S(1)}, f32[4,2048]{1,0:T(4,128)}, u32[]{:S(2)}) %copy-start.2) | copy-done | bytes 32792
  3.2 40.9 %shard_map.37 = f32[256,1024]{1,0:T(8,128)S(1)} custom-call(bf16[8,65536]{1,0:T(8,128)(2,1)S(1)} %copy-done, f32[4,2048]{1,0:T(4,128)S(1)} %copy-done.2, bf16[256,2048]{1,0:T(8,128)(2,1)S(1)} %copy-done.1), custom_call_target="tpu_custom_call" | custom-call | tf_op jit(solution)/shard_map/pallas_call | solution.py:276
  44.1 1.0 %copy.5 = f32[1,256,1024]{2,1,0:T(8,128)} copy(f32[1,256,1024]{2,1,0:T(8,128)S(1)} %bitcast.1) | data formatting | bytes 2097152
Async XLA Ops:
  0.0 1.2 %copy-start = (bf16[8,65536]{1,0:T(8,128)(2,1)S(1)}, bf16[8,65536]{1,0:T(8,128)(2,1)}, u32[]{:S(2)}) copy-start(bf16[8,65536]{1,0:T(8,128)(2,1)} %raw.1) | copy-start | bytes 3145732
  1.2 1.2 %copy-start.1 = (bf16[256,2048]{1,0:T(8,128)(2,1)S(1)}, bf16[256,2048]{1,0:T(8,128)(2,1)}, u32[]{:S(2)}) copy-start(bf16[256,2048]{1,0:T(8,128)(2,1)} %constant.2.clone.table) | copy-start | bytes 3145732
  2.5 0.8 %copy-start.2 = (f32[4,2048]{1,0:T(4,128)S(1)}, f32[4,2048]{1,0:T(4,128)}, u32[]{:S(2)}) copy-start(f32[4,2048]{1,0:T(4,128)} %taps.1) | copy-start | bytes 98308

commit v2 on v1

--- a/solution.py
+++ b/solution.py
@@ -15,6 +15,7 @@
 ALL_FRAMES = 128
 PLANE = 64
 LANES = 128
+TAIL = 8 * (TAPS - 1)
 CHUNK = 512
 SCALE = 1.0 / math.sqrt(NFFT)
 
@@ -42,27 +43,26 @@
     )
 
 
-def filter_frames(first, last, taps_v, raw_v, halo_v, filt_v):
+def filter_frames(first, last, taps_v, raw_v, filt_v):
     def step(c, carry):
         base = pl.multiple_of(c * CHUNK, CHUNK)
         taps = [taps_v[k : k + 1, pl.ds(base, CHUNK)] for k in range(TAPS)]
 
         def frame(f):
-            if f < 0:
-                ref, at = halo_v, (f + TAPS - 1) * NFFT
-            else:
-                ref, at = raw_v, f * NFFT
-            at = pl.multiple_of(base + at, CHUNK)
-            return ref[:, pl.ds(at, CHUNK)].astype(jnp.float32)
+            if not 0 <= f < FRAMES:
+                return None
+            at = pl.multiple_of(base + f * NFFT, CHUNK)
+            return raw_v[:, pl.ds(at, CHUNK)].astype(jnp.float32)
 
         window = [frame(first - k) for k in range(TAPS)]
         done = []
         for f in range(first, last):
             if f > first:
                 window = [frame(f)] + window[: TAPS - 1]
-            total = taps[0] * window[0]
-            for k in range(1, TAPS):
-                total = total + taps[k] * window[k]
+            total = jnp.zeros((8, CHUNK), jnp.float32)
+            for k in range(TAPS):
+                if window[k] is not None:
+                    total = total + taps[k] * window[k]
             done.append(total)
             if len(done) == 2:
                 pair = jnp.concatenate(done, axis=0).astype(jnp.bfloat16)
@@ -90,8 +90,8 @@
 
 def kernel(
     raw, taps, table, out,
-    raw_v, taps_v, table_v, halo_v, filt_v, sbuf, rbuf, xs, xr, lt,
-    in_sem, halo_ssem, halo_rsem, ssem, rsem, zssem, zrsem,
+    raw_v, taps_v, table_v, filt_v, tail_s, tail_r, sbuf, rbuf, xs, xr, lt,
+    in_sem, tail_ssem, tail_rsem, ssem, rsem, zssem, zrsem, fssem, frsem,
 ):
     me = lax.axis_index("inp")
     t = lax.axis_index("tm")
@@ -103,8 +103,8 @@
     def plane(d):
         return ((d // 8) * 16 + zh * 8 + d % 8, t)
 
-    def column(z):
-        return (y * 16 + (z // 4) * 8 + xc, z % 4)
+    def column(half, at):
+        return (y * 16 + half * 8 + xc, at)
 
     loads = [
         pltpu.make_async_copy(table, table_v, in_sem.at[0]),
@@ -117,7 +117,7 @@
     barrier = pltpu.get_barrier_semaphore()
     for k in range(1, 8):
         pl.semaphore_signal(
-            barrier, inc=1, device_id=column((my_z + k) % 8), device_id_type=MESH
+            barrier, inc=1, device_id=column((my_z + k) % 8 // 4, (my_z + k) % 4), device_id_type=MESH
         )
 
     def greet(k, carry):
@@ -127,36 +127,38 @@
         return carry
 
     lax.fori_loop(1, PLANE, greet, 0)
+    for load in loads:
+        load.wait()
+    filter_frames(FRAMES, FRAMES + 4, taps_v, raw_v, filt_v)
+    tail_s[...] = nt(filt_v[8 * FRAMES :, :], table_v[...])[:TAIL]
+    filter_frames(0, FRAMES, taps_v, raw_v, filt_v)
+    s0 = nt(table_v[...], filt_v[:LANES, :])
+    s1 = nt(table_v[...], filt_v[LANES : 2 * LANES, :])
+
     pl.semaphore_wait(barrier, PLANE - 1 + 7)
-
-    halo = pltpu.make_async_remote_copy(
-        src_ref=raw.at[:, pl.ds((FRAMES - TAPS + 1) * NFFT, (TAPS - 1) * NFFT)],
-        dst_ref=halo_v,
-        send_sem=halo_ssem,
-        recv_sem=halo_rsem,
+    tail = pltpu.make_async_remote_copy(
+        src_ref=tail_s,
+        dst_ref=tail_r,
+        send_sem=tail_ssem,
+        recv_sem=tail_rsem,
         device_id=(me, (t + 1) % 4),
         device_id_type=MESH,
     )
 
     @pl.when(t < 3)
     def _():
-        halo.start()
-
-    for load in loads:
-        load.wait()
-    filter_frames(4, FRAMES, taps_v, raw_v, halo_v, filt_v)
-    s1 = nt(table_v[...], filt_v[LANES:, :])
+        tail.start()
 
     @pl.when(t > 0)
     def _():
-        halo.wait_recv()
+        tail.wait_recv()
 
     @pl.when(t == 0)
     def _():
-        halo_v[...] = jnp.zeros_like(halo_v)
-
-    filter_frames(0, 4, taps_v, raw_v, halo_v, filt_v)
-    s0 = nt(table_v[...], filt_v[:LANES, :])
+        tail_r[...] = jnp.zeros_like(tail_r)
+
+    rest = jnp.zeros((LANES - TAIL, 4 * PLANE), jnp.float32)
+    s0 = s0 + jnp.concatenate([tail_r[...], rest], axis=0).T
     s0 = (s0 * SCALE).reshape(PLANE // 2, 8, LANES)
     s1 = (s1 * SCALE).reshape(PLANE // 2, 8, LANES)
     first = lax.broadcasted_iota(jnp.int32, (PLANE // 2, 8, LANES), 1) < 4
@@ -198,23 +200,57 @@
             for q in range(4):
                 pair = jnp.concatenate(halves[h][2 * q : 2 * q + 2], axis=0)
                 xs[m, h, 16 * q : 16 * q + 16, :] = pair.astype(jnp.bfloat16)
+        for end in (0, 3):
+            pltpu.make_async_remote_copy(
+                src_ref=xs.at[m, 1 - zh],
+                dst_ref=xr.at[m, my_z],
+                send_sem=zssem.at[m],
+                recv_sem=frsem.at[m],
+                device_id=column(1 - zh, end),
+                device_id_type=MESH,
+            ).start()
         pltpu.make_async_copy(xs.at[m, zh], xr.at[m, my_z], zrsem.at[m]).start()
-        for k in (4, 3, 5, 2, 6, 1, 7):
-            z = (my_z + k) % 8
+        for k in (2, 1, 3):
             pltpu.make_async_remote_copy(
-                src_ref=xs.at[m, z // 4],
+                src_ref=xs.at[m, zh],
                 dst_ref=xr.at[m, my_z],
                 send_sem=zssem.at[m],
                 recv_sem=zrsem.at[m],
-                device_id=column(z),
+                device_id=column(zh, (t + k) % 4),
                 device_id_type=MESH,
             ).start()
         return carry
 
     lax.fori_loop(0, 4, relay, 0)
 
+    is_end = jnp.logical_or(t == 0, t == 3)
+    theirs = pl.ds((1 - zh) * 4, 4)
+
+    def forward(m):
+        return pltpu.make_async_remote_copy(
+            src_ref=xr.at[m, theirs],
+            dst_ref=xr.at[m, theirs],
+            send_sem=fssem.at[m],
+            recv_sem=frsem.at[m],
+            device_id=column(zh, 1 + t // 3),
+            device_id_type=MESH,
+        )
+
+    def pass_on(j, carry):
+        m = (my_m - j + 4) % 4
+        pltpu.make_async_copy(xr.at[m, theirs], xr.at[m, theirs], frsem.at[m]).wait()
+
+        @pl.when(is_end)
+        def _():
+            forward(m).start()
+
+        return carry
+
+    lax.fori_loop(0, 4, pass_on, 0)
+
     for m in range(4):
-        pltpu.make_async_copy(xr.at[m], xr.at[m], zrsem.at[m]).wait()
+        half = xr.at[m, pl.ds(zh * 4, 4)]
+        pltpu.make_async_copy(half, half, zrsem.at[m]).wait()
 
     def block(m):
         both = [xr[m, 4 * z : 4 * z + 4].reshape(256, LANES) for z in range(2)]
@@ -262,13 +298,18 @@
 
     @pl.when(t < 3)
     def _():
-        halo.wait_send()
+        tail.wait_send()
 
     sent = rbuf.at[pl.ds(0, PLANE - 1)]
     pltpu.make_async_copy(sent, sent, ssem).wait()
     for m in range(4):
-        sent = xr.at[m, pl.ds(0, 7)]
+        sent = xr.at[m, pl.ds(0, 5)]
         pltpu.make_async_copy(sent, sent, zssem.at[m]).wait()
+
+    @pl.when(is_end)
+    def _():
+        for m in range(4):
+            forward(m).wait_send()
 
 
 def body(raw_samples, filter_taps):
@@ -282,8 +323,9 @@
             pltpu.VMEM((8, FRAMES * NFFT), jnp.bfloat16),
             pltpu.VMEM((TAPS, NFFT), jnp.float32),
             pltpu.VMEM((4 * PLANE, NFFT), jnp.bfloat16),
-            pltpu.VMEM((8, (TAPS - 1) * NFFT), jnp.bfloat16),
-            pltpu.VMEM((8 * FRAMES, NFFT), jnp.bfloat16),
+            pltpu.VMEM((8 * FRAMES + 32, NFFT), jnp.bfloat16),
+            pltpu.VMEM((TAIL, 4 * PLANE), jnp.float32),
+            pltpu.VMEM((TAIL, 4 * PLANE), jnp.float32),
             pltpu.VMEM((PLANE // 2, 2, 8, LANES), jnp.bfloat16),
             pltpu.VMEM((PLANE, 8, LANES), jnp.bfloat16),
             pltpu.VMEM((4, 2, 64, LANES), jnp.bfloat16),
@@ -296,9 +338,11 @@
             pltpu.SemaphoreType.DMA((4,)),
             pltpu.SemaphoreType.DMA((4,)),
             pltpu.SemaphoreType.DMA((4,)),
+            pltpu.SemaphoreType.DMA((4,)),
+            pltpu.SemaphoreType.DMA((4,)),
         ],
         compiler_params=pltpu.CompilerParams(
-            collective_id=0, has_side_effects=True, vmem_limit_bytes=40 << 20
+            collective_id=0, has_side_effects=True, vmem_limit_bytes=52 << 20
         ),
     )(raw_samples, filter_taps, jnp.asarray(table_rows()))
     return visibilities[None]

time: 45.3 us -> 39.5 us (0.87)
  the two profiles are of different devices: /device:TPU:1 before, /device:TPU:64 now
where the time goes in v2:
time: 39.5 us; the launch traced here: 39.4 us
  Pallas kernels  37.6 us (95%)
  local copies, waits for them, and re-layouts  1.73 us (4%)
    pallas_call x1, Pallas kernels, body(): pl.pallas_call(kernel, out_shape=jax.ShapeDtypeStruct((256, 1024), jnp.fl...  37.6 us
    unnamed x3, local copies, waits for them, and re-layouts  1.73 us

profile of v2, /device:TPU:64, one launch (start us, length us, event | category | flops | bytes accessed | tf_op | source)
XLA Modules:
  0.0 39.4 jit_solution(3049302550339241389)
XLA Ops:
  0.0 0.0 copy-start
  0.0 0.8 %copy-done = f32[4,2048]{1,0:T(4,128)S(1)} copy-done((f32[4,2048]{1,0:T(4,128)S(1)}, f32[4,2048]{1,0:T(4,128)}, u32[]{:S(2)}) %copy-start) | copy-done | bytes 32792
  0.8 37.6 %shard_map.37 = f32[256,1024]{1,0:T(8,128)S(1)} custom-call(bf16[8,65536]{1,0:T(8,128)(2,1)} %raw.1, f32[4,2048]{1,0:T(4,128)S(1)} %copy-done, bf16[256,2048]{1,0:T(8,128)(2,1)} %constant.2.clone.table), custom_call_target="tpu_custom_call" | custom-call | tf_op jit(solution)/shard_map/pallas_call | solution.py:317
  38.4 1.0 %copy.5 = f32[1,256,1024]{2,1,0:T(8,128)} copy(f32[1,256,1024]{2,1,0:T(8,128)S(1)} %bitcast.1) | data formatting | bytes 2097152
Async XLA Ops:
  0.0 0.8 %copy-start = (f32[4,2048]{1,0:T(4,128)S(1)}, f32[4,2048]{1,0:T(4,128)}, u32[]{:S(2)}) copy-start(f32[4,2048]{1,0:T(4,128)} %taps.1) | copy-start | bytes 98308

commit v3 on v2

--- a/solution.py
+++ b/solution.py
@@ -29,6 +29,10 @@
     angles = m.astype(np.float32) * np.float32(2.0 * math.pi / NFFT)
     rows = np.where(part[:, None] == 0, np.cos(angles), -np.sin(angles))
     return rows.astype(np.float32).astype(jnp.bfloat16)
+
+
+def hops(dy, dc, dz=0):
+    return min(dy, 8 - dy) + min(dc // 2, 4 - dc // 2) + min(dz, 8 - dz)
 
 
 def nt(left, right):
@@ -91,17 +95,16 @@
 def kernel(
     raw, taps, table, out,
     raw_v, taps_v, table_v, filt_v, tail_s, tail_r, sbuf, rbuf, xs, xr, lt,
-    in_sem, tail_ssem, tail_rsem, ssem, rsem, zssem, zrsem, fssem, frsem,
+    in_sem, tail_ssem, tail_rsem, ssem, rsem, zssem, zrsem, cssem, fssem, frsem, vouch,
 ):
     me = lax.axis_index("inp")
     t = lax.axis_index("tm")
     y, zh, xc = me // 16, (me // 8) % 2, me % 8
     mine = y * 8 + xc
-    my_m, my_lo = mine // 16, mine % 16
-    my_z = zh * 4 + t
-
-    def plane(d):
-        return ((d // 8) * 16 + zh * 8 + d % 8, t)
+    my_m, my_z = mine // 16, zh * 4 + t
+
+    def beside(dc):
+        return (xc // 2 + dc // 2) % 4 * 2 + (xc + dc) % 2
 
     def column(half, at):
         return (y * 16 + half * 8 + xc, at)
@@ -115,18 +118,13 @@
         load.start()
 
     barrier = pltpu.get_barrier_semaphore()
-    for k in range(1, 8):
-        pl.semaphore_signal(
-            barrier, inc=1, device_id=column((my_z + k) % 8 // 4, (my_z + k) % 4), device_id_type=MESH
-        )
-
-    def greet(k, carry):
-        pl.semaphore_signal(
-            barrier, inc=1, device_id=plane((mine + k) % PLANE), device_id_type=MESH
-        )
-        return carry
-
-    lax.fori_loop(1, PLANE, greet, 0)
+    offsets = [(0, 0, dz) for dz in range(1, 8)] + [(0, 1, 0)]
+    offsets += [(dy, 2 * dx, 0) for dy in range(8) for dx in range(4) if dy + dx]
+    for dy, dc, dz in sorted(offsets, key=lambda o: -hops(*o)):
+        z = (my_z + dz) % 8
+        peer = (((y + dy) % 8) * 16 + (z // 4) * 8 + beside(dc), z % 4)
+        pl.semaphore_signal(barrier, inc=1, device_id=peer, device_id_type=MESH)
+
     for load in loads:
         load.wait()
     filter_frames(FRAMES, FRAMES + 4, taps_v, raw_v, filt_v)
@@ -135,7 +133,9 @@
     s0 = nt(table_v[...], filt_v[:LANES, :])
     s1 = nt(table_v[...], filt_v[LANES : 2 * LANES, :])
 
-    pl.semaphore_wait(barrier, PLANE - 1 + 7)
+    pl.semaphore_wait(barrier, 39)
+    partner = (y * 16 + zh * 8 + beside(1), t)
+    pl.semaphore_signal(vouch, inc=1, device_id=partner, device_id_type=MESH)
     tail = pltpu.make_async_remote_copy(
         src_ref=tail_s,
         dst_ref=tail_r,
@@ -165,26 +165,53 @@
     sbuf[:, 0] = jnp.where(first, s0, pltpu.roll(s1, 4, 1)).astype(jnp.bfloat16)
     sbuf[:, 1] = jnp.where(first, pltpu.roll(s0, 4, 1), s1).astype(jnp.bfloat16)
 
+    pl.semaphore_wait(vouch, 1)
     own = pltpu.make_async_copy(
         sbuf.at[mine // 2, mine % 2], rbuf.at[mine], rsem.at[my_m]
     )
     own.start()
 
-    def send(k, carry):
-        d = ((my_m + k // 16) % 4) * 16 + (my_lo + k % 16) % 16
-        pltpu.make_async_remote_copy(
-            src_ref=sbuf.at[d // 2, d % 2],
-            dst_ref=rbuf.at[mine],
-            send_sem=ssem,
-            recv_sem=rsem.at[my_m],
-            device_id=plane(d),
-            device_id_type=MESH,
-        ).start()
-        return carry
-
-    lax.fori_loop(1, PLANE, send, 0)
+    order = [(p, dc) for p in range(2) for dc in range(8)]
+    order.sort(key=lambda o: -hops(*o))
+    for j in range(4):
+        for p, dc in order:
+            if j + p + dc == 0:
+                continue
+            to_y = (my_m + j) % 4 * 2 + (y + p) % 2
+            to = beside(dc)
+            pltpu.make_async_remote_copy(
+                src_ref=sbuf.at[to_y * 4 + to // 2, to % 2],
+                dst_ref=rbuf.at[mine],
+                send_sem=ssem,
+                recv_sem=rsem.at[my_m],
+                device_id=(to_y * 16 + zh * 8 + to, t),
+                device_id_type=MESH,
+            ).start()
 
     sub = lax.broadcasted_iota(jnp.int32, (8, LANES), 0)
+
+    def cross(m):
+        for end in (3, 0):
+            pltpu.make_async_remote_copy(
+                src_ref=xs.at[m, 1 - zh],
+                dst_ref=xr.at[m, my_z],
+                send_sem=cssem.at[m],
+                recv_sem=frsem.at[m * 2 + t // 2],
+                device_id=column(1 - zh, end),
+                device_id_type=MESH,
+            ).start()
+
+    def share(m):
+        pltpu.make_async_copy(xs.at[m, zh], xr.at[m, my_z], zrsem.at[m]).start()
+        for k in (2, 1, 3):
+            pltpu.make_async_remote_copy(
+                src_ref=xs.at[m, zh],
+                dst_ref=xr.at[m, my_z],
+                send_sem=zssem.at[m],
+                recv_sem=zrsem.at[m],
+                device_id=column(zh, (t + k) % 4),
+                device_id_type=MESH,
+            ).start()
 
     def relay(j, carry):
         m = (my_m - j + 4) % 4
@@ -200,49 +227,68 @@
             for q in range(4):
                 pair = jnp.concatenate(halves[h][2 * q : 2 * q + 2], axis=0)
                 xs[m, h, 16 * q : 16 * q + 16, :] = pair.astype(jnp.bfloat16)
-        for end in (0, 3):
-            pltpu.make_async_remote_copy(
-                src_ref=xs.at[m, 1 - zh],
-                dst_ref=xr.at[m, my_z],
-                send_sem=zssem.at[m],
-                recv_sem=frsem.at[m],
-                device_id=column(1 - zh, end),
-                device_id_type=MESH,
-            ).start()
-        pltpu.make_async_copy(xs.at[m, zh], xr.at[m, my_z], zrsem.at[m]).start()
-        for k in (2, 1, 3):
-            pltpu.make_async_remote_copy(
-                src_ref=xs.at[m, zh],
-                dst_ref=xr.at[m, my_z],
-                send_sem=zssem.at[m],
-                recv_sem=zrsem.at[m],
-                device_id=column(zh, (t + k) % 4),
-                device_id_type=MESH,
-            ).start()
+
+        @pl.when(zh == 0)
+        def _():
+            share(m)
+
+        @pl.when(zh == 1)
+        def _():
+            cross(m)
+
         return carry
 
     lax.fori_loop(0, 4, relay, 0)
 
+    def drain_cross():
+        for m in range(4):
+            sent = xr.at[m, pl.ds(0, 2)]
+            pltpu.make_async_copy(sent, sent, cssem.at[m]).wait()
+
+    def rest(j, carry):
+        m = (my_m - j + 4) % 4
+
+        @pl.when(zh == 0)
+        def _():
+            cross(m)
+
+        @pl.when(zh == 1)
+        def _():
+            share(m)
+
+        return carry
+
+    @pl.when(zh == 1)
+    def _():
+        drain_cross()
+
+    lax.fori_loop(0, 4, rest, 0)
+
     is_end = jnp.logical_or(t == 0, t == 3)
-    theirs = pl.ds((1 - zh) * 4, 4)
-
-    def forward(m):
+    nearer = 1 - t // 2
+
+    def pair(m, which):
+        return xr.at[m, pl.ds((1 - zh) * 4 + which * 2, 2)]
+
+    def forward(m, inner):
         return pltpu.make_async_remote_copy(
-            src_ref=xr.at[m, theirs],
-            dst_ref=xr.at[m, theirs],
+            src_ref=pair(m, nearer),
+            dst_ref=pair(m, nearer),
             send_sem=fssem.at[m],
-            recv_sem=frsem.at[m],
-            device_id=column(zh, 1 + t // 3),
+            recv_sem=frsem.at[m * 2 + nearer],
+            device_id=column(zh, inner),
             device_id_type=MESH,
         )
 
     def pass_on(j, carry):
         m = (my_m - j + 4) % 4
-        pltpu.make_async_copy(xr.at[m, theirs], xr.at[m, theirs], frsem.at[m]).wait()
+        got = pair(m, nearer)
+        pltpu.make_async_copy(got, got, frsem.at[m * 2 + nearer]).wait()
 
         @pl.when(is_end)
         def _():
-            forward(m).start()
+            forward(m, 2 - t // 3).start()
+            forward(m, 1 + t // 3).start()
 
         return carry
 
@@ -251,6 +297,8 @@
     for m in range(4):
         half = xr.at[m, pl.ds(zh * 4, 4)]
         pltpu.make_async_copy(half, half, zrsem.at[m]).wait()
+        got = pair(m, 1 - nearer)
+        pltpu.make_async_copy(got, got, frsem.at[m * 2 + 1 - nearer]).wait()
 
     def block(m):
         both = [xr[m, 4 * z : 4 * z + 4].reshape(256, LANES) for z in range(2)]
@@ -303,13 +351,18 @@
     sent = rbuf.at[pl.ds(0, PLANE - 1)]
     pltpu.make_async_copy(sent, sent, ssem).wait()
     for m in range(4):
-        sent = xr.at[m, pl.ds(0, 5)]
+        sent = xr.at[m, pl.ds(0, 3)]
         pltpu.make_async_copy(sent, sent, zssem.at[m]).wait()
 
+    @pl.when(zh == 0)
+    def _():
+        drain_cross()
+
     @pl.when(is_end)
     def _():
         for m in range(4):
-            forward(m).wait_send()
+            sent = xr.at[m, pl.ds(0, 4)]
+            pltpu.make_async_copy(sent, sent, fssem.at[m]).wait()
 
 
 def body(raw_samples, filter_taps):
@@ -340,11 +393,13 @@
             pltpu.SemaphoreType.DMA((4,)),
             pltpu.SemaphoreType.DMA((4,)),
             pltpu.SemaphoreType.DMA((4,)),
+            pltpu.SemaphoreType.DMA((8,)),
+            pltpu.SemaphoreType.REGULAR,
         ],
         compiler_params=pltpu.CompilerParams(
             collective_id=0, has_side_effects=True, vmem_limit_bytes=52 << 20
         ),
-    )(raw_samples, filter_taps, jnp.asarray(table_rows()))
+    )(raw_samples, pltpu.with_memory_space_constraint(filter_taps, pltpu.HBM), jnp.asarray(table_rows()))
     return visibilities[None]
 
 

time: 39.5 us -> 37.9 us (0.959)
  Pallas kernels: 37.6 us -> 36.8 us
  local copies, waits for them, and re-layouts: 1.73 us -> 0.97 us
    pallas_call x1, Pallas kernels: 37.6 us -> 36.8 us  [body(): pl.pallas_call(kernel, out_shape=jax.ShapeDtypeStruct((256, 1024), jnp.fl...]
    unnamed x3 -> x1, local copies, waits for them, and re-layouts: 1.73 us -> 0.97 us
where the time goes in v3:
time: 37.9 us; the launch traced here: 37.8 us
  Pallas kernels  36.8 us (97%)
  local copies, waits for them, and re-layouts  0.97 us (3%)
    pallas_call x1, Pallas kernels, body(): pl.pallas_call(kernel, out_shape=jax.ShapeDtypeStruct((256, 1024), jnp.fl...  36.8 us
    unnamed x1, local copies, waits for them, and re-layouts  0.97 us

profile of v3, /device:TPU:64, one launch (start us, length us, event | category | flops | bytes accessed | tf_op | source)
XLA Modules:
  0.0 37.8 jit_solution(8627444436534870574)
XLA Ops:
  0.0 36.8 %shard_map.37 = f32[256,1024]{1,0:T(8,128)S(1)} custom-call(bf16[8,65536]{1,0:T(8,128)(2,1)} %raw.1, f32[4,2048]{1,0:T(4,128)} %taps.1, bf16[256,2048]{1,0:T(8,128)(2,1)} %constant.2.clone.table), custom_call_target="tpu_custom_call" | custom-call | tf_op jit(solution)/shard_map/pallas_call | solution.py:370
  36.8 1.0 %copy.5 = f32[1,256,1024]{2,1,0:T(8,128)} copy(f32[1,256,1024]{2,1,0:T(8,128)S(1)} %bitcast.1) | data formatting | bytes 2097152

commit v4 on v3

--- a/solution.py
+++ b/solution.py
@@ -17,13 +17,15 @@
 LANES = 128
 TAIL = 8 * (TAPS - 1)
 CHUNK = 512
+STEPS = (0, 1, 2, 3)
 SCALE = 1.0 / math.sqrt(NFFT)
 
 
 def table_rows():
     row = np.arange(4 * PLANE)
-    part, z_hi, dest = row % 2, row // 2 % 2, row // 4
-    channel = ((dest // 8) * 2 + z_hi) * 8 + dest % 8
+    part, core, dest = row % 2, row // 2 % 2, row // 4
+    y, x, z_hi = dest // 8, dest // 2 % 4, dest % 2
+    channel = ((y * 2 + z_hi) * 4 + x) * 2 + core
     n = np.arange(NFFT)
     m = (n[None, :] * (channel[:, None] + 1)) % NFFT
     angles = m.astype(np.float32) * np.float32(2.0 * math.pi / NFFT)
@@ -106,8 +108,10 @@
     def beside(dc):
         return (xc // 2 + dc // 2) % 4 * 2 + (xc + dc) % 2
 
-    def column(half, at):
-        return (y * 16 + half * 8 + xc, at)
+    core = xc % 2
+
+    def column(half, at, of=core):
+        return (y * 16 + half * 8 + xc - core + of, at)
 
     loads = [
         pltpu.make_async_copy(table, table_v, in_sem.at[0]),
@@ -118,8 +122,8 @@
         load.start()
 
     barrier = pltpu.get_barrier_semaphore()
-    offsets = [(0, 0, dz) for dz in range(1, 8)] + [(0, 1, 0)]
-    offsets += [(dy, 2 * dx, 0) for dy in range(8) for dx in range(4) if dy + dx]
+    offsets = [(0, 0, dz) for dz in range(1, 8)] + [(dy, 0, 0) for dy in range(1, 8)]
+    offsets += [(0, dc, 0) for dc in range(1, 8)]
     for dy, dc, dz in sorted(offsets, key=lambda o: -hops(*o)):
         z = (my_z + dz) % 8
         peer = (((y + dy) % 8) * 16 + (z // 4) * 8 + beside(dc), z % 4)
@@ -129,13 +133,9 @@
         load.wait()
     filter_frames(FRAMES, FRAMES + 4, taps_v, raw_v, filt_v)
     tail_s[...] = nt(filt_v[8 * FRAMES :, :], table_v[...])[:TAIL]
-    filter_frames(0, FRAMES, taps_v, raw_v, filt_v)
-    s0 = nt(table_v[...], filt_v[:LANES, :])
-    s1 = nt(table_v[...], filt_v[LANES : 2 * LANES, :])
-
-    pl.semaphore_wait(barrier, 39)
+
+    pl.semaphore_wait(barrier, 21)
     partner = (y * 16 + zh * 8 + beside(1), t)
-    pl.semaphore_signal(vouch, inc=1, device_id=partner, device_id_type=MESH)
     tail = pltpu.make_async_remote_copy(
         src_ref=tail_s,
         dst_ref=tail_r,
@@ -149,6 +149,14 @@
     def _():
         tail.start()
 
+    for dc in (4, 5, 2, 3, 6, 7, 1):
+        peer = (y * 16 + zh * 8 + beside(dc), t)
+        pl.semaphore_signal(vouch, inc=1, device_id=peer, device_id_type=MESH)
+
+    filter_frames(0, FRAMES, taps_v, raw_v, filt_v)
+    both = nt(table_v[...], filt_v[: 2 * LANES, :])
+    s0, s1 = both[:, :LANES], both[:, LANES:]
+
     @pl.when(t > 0)
     def _():
         tail.wait_recv()
@@ -165,53 +173,59 @@
     sbuf[:, 0] = jnp.where(first, s0, pltpu.roll(s1, 4, 1)).astype(jnp.bfloat16)
     sbuf[:, 1] = jnp.where(first, pltpu.roll(s0, 4, 1), s1).astype(jnp.bfloat16)
 
-    pl.semaphore_wait(vouch, 1)
+    pl.semaphore_wait(vouch, 7)
     own = pltpu.make_async_copy(
         sbuf.at[mine // 2, mine % 2], rbuf.at[mine], rsem.at[my_m]
     )
     own.start()
 
-    order = [(p, dc) for p in range(2) for dc in range(8)]
-    order.sort(key=lambda o: -hops(*o))
-    for j in range(4):
-        for p, dc in order:
-            if j + p + dc == 0:
-                continue
-            to_y = (my_m + j) % 4 * 2 + (y + p) % 2
-            to = beside(dc)
-            pltpu.make_async_remote_copy(
-                src_ref=sbuf.at[to_y * 4 + to // 2, to % 2],
-                dst_ref=rbuf.at[mine],
-                send_sem=ssem,
-                recv_sem=rsem.at[my_m],
-                device_id=(to_y * 16 + zh * 8 + to, t),
-                device_id_type=MESH,
-            ).start()
+    def send(to_y, to):
+        pltpu.make_async_remote_copy(
+            src_ref=sbuf.at[to_y * 4 + to // 2, to % 2],
+            dst_ref=rbuf.at[mine],
+            send_sem=ssem,
+            recv_sem=rsem.at[my_m],
+            device_id=(to_y * 16 + zh * 8 + to, t),
+            device_id_type=MESH,
+        ).start()
+
+    order = [(p, dx) for p in range(2) for dx in range(4)]
+    order.sort(key=lambda o: -hops(o[0], 2 * o[1]))
+    for h in range(2):
+        for j in STEPS:
+            for p, dx in order:
+                if j + p + dx:
+                    to_y = (my_m + j) % 4 * 2 + (y + p) % 2
+                    send(to_y, (xc // 2 + dx) % 4 * 2 + h)
+        if h == 0:
+            send(y, beside(1))
 
     sub = lax.broadcasted_iota(jnp.int32, (8, LANES), 0)
 
-    def cross(m):
-        for end in (3, 0):
-            pltpu.make_async_remote_copy(
-                src_ref=xs.at[m, 1 - zh],
-                dst_ref=xr.at[m, my_z],
-                send_sem=cssem.at[m],
-                recv_sem=frsem.at[m * 2 + t // 2],
-                device_id=column(1 - zh, end),
-                device_id_type=MESH,
-            ).start()
+    def copy_block(m, of, to, send_sem, recv_sem):
+        pltpu.make_async_remote_copy(
+            src_ref=xs.at[m, of],
+            dst_ref=xr.at[m, my_z],
+            send_sem=send_sem,
+            recv_sem=recv_sem,
+            device_id=to,
+            device_id_type=MESH,
+        ).start()
+
+    def cross(m, end):
+        for of in range(2):
+            to = column(1 - zh, end, of)
+            copy_block(m, of, to, cssem.at[m], frsem.at[m * 2 + t // 2])
 
     def share(m):
-        pltpu.make_async_copy(xs.at[m, zh], xr.at[m, my_z], zrsem.at[m]).start()
+        pltpu.make_async_copy(xs.at[m, core], xr.at[m, my_z], zrsem.at[m]).start()
+        copy_block(m, 1 - core, partner, zssem.at[m], zrsem.at[m])
         for k in (2, 1, 3):
-            pltpu.make_async_remote_copy(
-                src_ref=xs.at[m, zh],
-                dst_ref=xr.at[m, my_z],
-                send_sem=zssem.at[m],
-                recv_sem=zrsem.at[m],
-                device_id=column(zh, (t + k) % 4),
-                device_id_type=MESH,
-            ).start()
+            for of in range(2):
+                to = column(zh, (t + k) % 4, of)
+                copy_block(m, of, to, zssem.at[m], zrsem.at[m])
+
+    near = 3 - t // 2 * 3
 
     def relay(j, carry):
         m = (my_m - j + 4) % 4
@@ -228,41 +242,18 @@
                 pair = jnp.concatenate(halves[h][2 * q : 2 * q + 2], axis=0)
                 xs[m, h, 16 * q : 16 * q + 16, :] = pair.astype(jnp.bfloat16)
 
-        @pl.when(zh == 0)
+        @pl.when(core == zh)
         def _():
             share(m)
 
-        @pl.when(zh == 1)
+        @pl.when(core != zh)
         def _():
-            cross(m)
+            cross(m, near)
+            cross(m, 3 - near)
 
         return carry
 
     lax.fori_loop(0, 4, relay, 0)
-
-    def drain_cross():
-        for m in range(4):
-            sent = xr.at[m, pl.ds(0, 2)]
-            pltpu.make_async_copy(sent, sent, cssem.at[m]).wait()
-
-    def rest(j, carry):
-        m = (my_m - j + 4) % 4
-
-        @pl.when(zh == 0)
-        def _():
-            cross(m)
-
-        @pl.when(zh == 1)
-        def _():
-            share(m)
-
-        return carry
-
-    @pl.when(zh == 1)
-    def _():
-        drain_cross()
-
-    lax.fori_loop(0, 4, rest, 0)
 
     is_end = jnp.logical_or(t == 0, t == 3)
     nearer = 1 - t // 2
@@ -342,7 +333,8 @@
         put(m, nn(lt[(m < t).astype(jnp.int32)], block(m)))
         return carry
 
-    lax.fori_loop(1, 4, other, 0)
+    for j in range(1, 4):
+        other(j, 0)
 
     @pl.when(t < 3)
     def _():
@@ -350,13 +342,17 @@
 
     sent = rbuf.at[pl.ds(0, PLANE - 1)]
     pltpu.make_async_copy(sent, sent, ssem).wait()
-    for m in range(4):
-        sent = xr.at[m, pl.ds(0, 3)]
-        pltpu.make_async_copy(sent, sent, zssem.at[m]).wait()
-
-    @pl.when(zh == 0)
-    def _():
-        drain_cross()
+    @pl.when(core == zh)
+    def _():
+        for m in range(4):
+            sent = xr.at[m, pl.ds(0, 7)]
+            pltpu.make_async_copy(sent, sent, zssem.at[m]).wait()
+
+    @pl.when(core != zh)
+    def _():
+        for m in range(4):
+            sent = xr.at[m, pl.ds(0, 4)]
+            pltpu.make_async_copy(sent, sent, cssem.at[m]).wait()
 
     @pl.when(is_end)
     def _():

time: 37.9 us -> 36.2 us (0.955)
  the two profiles are of different devices: /device:TPU:64 before, /device:TPU:1 now
where the time goes in v4:
time: 36.2 us; the launch traced here: 36 us
  Pallas kernels  35 us (97%)
  local copies, waits for them, and re-layouts  0.97 us (3%)
    pallas_call x1, Pallas kernels, body(): pl.pallas_call(kernel, out_shape=jax.ShapeDtypeStruct((256, 1024), jnp.fl...  35 us
    unnamed x1, local copies, waits for them, and re-layouts  0.97 us

profile of v4, /device:TPU:1, one launch (start us, length us, event | category | flops | bytes accessed | tf_op | source)
XLA Modules:
  0.0 36.0 jit_solution(13423315682768544013)
XLA Ops:
  0.0 35.0 %shard_map.37 = f32[256,1024]{1,0:T(8,128)S(1)} custom-call(bf16[8,65536]{1,0:T(8,128)(2,1)} %raw.1, f32[4,2048]{1,0:T(4,128)} %taps.1, bf16[256,2048]{1,0:T(8,128)(2,1)} %constant.2.clone.table), custom_call_target="tpu_custom_call" | custom-call | tf_op jit(solution)/shard_map/pallas_call | solution.py:366
  35.0 1.0 %copy.5 = f32[1,256,1024]{2,1,0:T(8,128)} copy(f32[1,256,1024]{2,1,0:T(8,128)S(1)} %bitcast.1) | data formatting | bytes 2097152

commit v5 on v4

--- a/solution.py
+++ b/solution.py
@@ -17,7 +17,7 @@
 LANES = 128
 TAIL = 8 * (TAPS - 1)
 CHUNK = 512
-STEPS = (0, 1, 2, 3)
+STEPS = (0, 3, 2, 1)
 SCALE = 1.0 / math.sqrt(NFFT)
 
 
@@ -228,10 +228,11 @@
     near = 3 - t // 2 * 3
 
     def relay(j, carry):
-        m = (my_m - j + 4) % 4
+        m = (my_m + j) % 4
         got = rbuf.at[pl.ds(m * 16, 16)]
         pltpu.make_async_copy(got, got, rsem.at[m]).wait()
-        rows = turn([rbuf[m * 16 + s].astype(jnp.float32) for s in range(16)])
+        at = [m * 16 + (s // 8 + zh) % 2 * 8 + s % 8 for s in range(16)]
+        rows = turn([rbuf[s].astype(jnp.float32) for s in at])
         halves = ([], [])
         for p in range(8):
             a, b = rows[2 * p], rows[2 * p + 1]
@@ -272,7 +273,7 @@
         )
 
     def pass_on(j, carry):
-        m = (my_m - j + 4) % 4
+        m = (my_m + j) % 4
         got = pair(m, nearer)
         pltpu.make_async_copy(got, got, frsem.at[m * 2 + nearer]).wait()
 
@@ -291,9 +292,15 @@
         got = pair(m, 1 - nearer)
         pltpu.make_async_copy(got, got, frsem.at[m * 2 + 1 - nearer]).wait()
 
+    low = lax.broadcasted_iota(jnp.int32, (256, LANES), 1) < 64
+
     def block(m):
-        both = [xr[m, 4 * z : 4 * z + 4].reshape(256, LANES) for z in range(2)]
-        return jnp.concatenate(both, axis=1)
+        x, y = [
+            xr[m, 4 * z : 4 * z + 4].reshape(256, LANES).astype(jnp.float32)
+            for z in range(2)
+        ]
+        tiles = [jnp.where(low, x, y), pltpu.roll(jnp.where(low, y, x), 64, 1)]
+        return jnp.concatenate(tiles, axis=1).astype(jnp.bfloat16)
 
     held = block(t).astype(jnp.float32)
     grouped = held.reshape(32, 8, 256)
@@ -302,30 +309,13 @@
     lt[0] = held.T.astype(jnp.bfloat16)
     lt[1] = swapped.reshape(256, 256).T.astype(jnp.bfloat16)
 
-    lane = lax.broadcasted_iota(jnp.int32, (256, LANES), 1)
-
     def put(m, packed):
-        packed = packed * (1.0 / ALL_FRAMES)
-        a, b = packed[:, :LANES], packed[:, LANES:]
         base = pl.multiple_of(m * 256, 256)
-        tiles = (
-            jnp.where(lane < 64, a, pltpu.roll(b, 64, 1)),
-            jnp.where(lane < 64, pltpu.roll(a, 64, 1), b),
-        )
-        for part, tile in enumerate(tiles):
-            for z in range(2):
-                for half in range(2):
-                    out[
-                        half * 128 + z * 64 : half * 128 + z * 64 + 64,
-                        pl.ds(base + part * LANES, LANES),
-                    ] = tile[z * 128 + half * 64 : z * 128 + half * 64 + 64]
-
-    def place(index):
-        return (index // 64 % 2) * 128 + (index // 128) * 64 + index % 64
+        out[:, pl.ds(base, 256)] = packed * (1.0 / ALL_FRAMES)
 
     right = block(t)
-    row = place(lax.broadcasted_iota(jnp.int32, (256, 256), 0))
-    col = place(lax.broadcasted_iota(jnp.int32, (256, 256), 1))
+    row = lax.broadcasted_iota(jnp.int32, (256, 256), 0)
+    col = lax.broadcasted_iota(jnp.int32, (256, 256), 1)
     put(t, jnp.where(row <= col, nn(lt[0], right), nn(lt[1], right)))
 
     def other(j, carry):

time: 36.2 us -> 35.7 us (0.986)
  Pallas kernels: 35 us -> 34.6 us
    pallas_call x1, Pallas kernels: 35 us -> 34.6 us  [body(): pl.pallas_call(kernel, out_shape=jax.ShapeDtypeStruct((256, 1024), jnp.fl...]
where the time goes in v5:
time: 35.7 us; the launch traced here: 35.6 us
  Pallas kernels  34.6 us (97%)
  local copies, waits for them, and re-layouts  0.97 us (3%)
    pallas_call x1, Pallas kernels, body(): pl.pallas_call(kernel, out_shape=jax.ShapeDtypeStruct((256, 1024), jnp.fl...  34.6 us
    unnamed x1, local copies, waits for them, and re-layouts  0.97 us

profile of v5, /device:TPU:1, one launch (start us, length us, event | category | flops | bytes accessed | tf_op | source)
XLA Modules:
  0.0 35.6 jit_solution(17068444702218673857)
XLA Ops:
  0.0 34.6 %shard_map.37 = f32[256,1024]{1,0:T(8,128)S(1)} custom-call(bf16[8,65536]{1,0:T(8,128)(2,1)} %raw.1, f32[4,2048]{1,0:T(4,128)} %taps.1, bf16[256,2048]{1,0:T(8,128)(2,1)} %constant.2.clone.table), custom_call_target="tpu_custom_call" | custom-call | tf_op jit(solution)/shard_map/pallas_call | solution.py:356
  34.6 1.0 %copy.5 = f32[1,256,1024]{2,1,0:T(8,128)} copy(f32[1,256,1024]{2,1,0:T(8,128)S(1)} %bitcast.1) | data formatting | bytes 2097152

commit v6 on v5

--- a/solution.py
+++ b/solution.py
@@ -114,9 +114,9 @@
         return (y * 16 + half * 8 + xc - core + of, at)
 
     loads = [
-        pltpu.make_async_copy(table, table_v, in_sem.at[0]),
         pltpu.make_async_copy(taps, taps_v, in_sem.at[1]),
         pltpu.make_async_copy(raw, raw_v, in_sem.at[2]),
+        pltpu.make_async_copy(table, table_v, in_sem.at[0]),
     ]
     for load in loads:
         load.start()
@@ -129,9 +129,10 @@
         peer = (((y + dy) % 8) * 16 + (z // 4) * 8 + beside(dc), z % 4)
         pl.semaphore_signal(barrier, inc=1, device_id=peer, device_id_type=MESH)
 
-    for load in loads:
-        load.wait()
+    loads[0].wait()
+    loads[1].wait()
     filter_frames(FRAMES, FRAMES + 4, taps_v, raw_v, filt_v)
+    loads[2].wait()
     tail_s[...] = nt(filt_v[8 * FRAMES :, :], table_v[...])[:TAIL]
 
     pl.semaphore_wait(barrier, 21)
@@ -156,6 +157,8 @@
     filter_frames(0, FRAMES, taps_v, raw_v, filt_v)
     both = nt(table_v[...], filt_v[: 2 * LANES, :])
     s0, s1 = both[:, :LANES], both[:, LANES:]
+    s1 = (s1 * SCALE).reshape(PLANE // 2, 8, LANES)
+    s1_turned = pltpu.roll(s1, 4, 1)
 
     @pl.when(t > 0)
     def _():
@@ -168,9 +171,8 @@
     rest = jnp.zeros((LANES - TAIL, 4 * PLANE), jnp.float32)
     s0 = s0 + jnp.concatenate([tail_r[...], rest], axis=0).T
     s0 = (s0 * SCALE).reshape(PLANE // 2, 8, LANES)
-    s1 = (s1 * SCALE).reshape(PLANE // 2, 8, LANES)
     first = lax.broadcasted_iota(jnp.int32, (PLANE // 2, 8, LANES), 1) < 4
-    sbuf[:, 0] = jnp.where(first, s0, pltpu.roll(s1, 4, 1)).astype(jnp.bfloat16)
+    sbuf[:, 0] = jnp.where(first, s0, s1_turned).astype(jnp.bfloat16)
     sbuf[:, 1] = jnp.where(first, pltpu.roll(s0, 4, 1), s1).astype(jnp.bfloat16)
 
     pl.semaphore_wait(vouch, 7)

time: 35.7 us -> 35.7 us (level)
  no operation moved by 1% of the time
where the time goes in v6:
time: 35.7 us; the launch traced here: 35.6 us
  Pallas kernels  34.6 us (97%)
  local copies, waits for them, and re-layouts  0.97 us (3%)
    pallas_call x1, Pallas kernels, body(): pl.pallas_call(kernel, out_shape=jax.ShapeDtypeStruct((256, 1024), jnp.fl...  34.6 us
    unnamed x1, local copies, waits for them, and re-layouts  0.97 us

profile of v6, /device:TPU:1, one launch (start us, length us, event | category | flops | bytes accessed | tf_op | source)
XLA Modules:
  0.0 35.6 jit_solution(5070940397714383843)
XLA Ops:
  0.0 34.6 %shard_map.37 = f32[256,1024]{1,0:T(8,128)S(1)} custom-call(bf16[8,65536]{1,0:T(8,128)(2,1)} %raw.1, f32[4,2048]{1,0:T(4,128)} %taps.1, bf16[256,2048]{1,0:T(8,128)(2,1)} %constant.2.clone.table), custom_call_target="tpu_custom_call" | custom-call | tf_op jit(solution)/shard_map/pallas_call | solution.py:358
  34.6 1.0 %copy.5 = f32[1,256,1024]{2,1,0:T(8,128)} copy(f32[1,256,1024]{2,1,0:T(8,128)S(1)} %bitcast.1) | data formatting | bytes 2097152
